TPU v7x, 256 devices: a whole 4x4x8 slice. The times are simulated.
256 devices in a mesh: freq: 16 (over x, y_hi, core), src: 16 (over y_lo, z).
Axes of the slice: x: 4, y: 4 (y_hi: 2, y_lo: 2; y = y_hi * 2 + y_lo), z: 8, core: 2. Of those that a mesh axis runs over, the one named last changes fastest.
Arguments:
- response: bfloat16 [2, 32, 4096, 4096], P(None, 'freq', 'src'), may hold values from -0.09375 to 0.09375
- focus_plus: bfloat16 [192, 256, 4096], P('freq', None, 'src'), may hold values from -6 to 6
- onset: int32 [192, 4096], P('freq', 'src'), may hold values from 64 to 255
Outputs:
- focus_minus: bfloat16 [192, 256, 4096], P('freq', None, 'src')
Inputs may be any that keep to these rules, and one draw needn't show every extreme that they name: onset[x, s] is the first time sample of the direct arrival from position s to focal point x.
All inputs are finite; a program needn't handle non-finite values.
Results may differ from a plain program's by a relative error of at most 0.0066.
Values may be sent and summed in bfloat16 or wider, within the bound.
A program may use at most 128 MiB of HBM per device.

v0:
```python
import math

import jax
import jax.numpy as jnp
from jax import lax
from jax.sharding import PartitionSpec as P


def phase_angle(first, count, samples):
    bins = first + jnp.arange(count, dtype=jnp.int32) + 1
    times = jnp.arange(samples, dtype=jnp.int32)
    phase = times[:, None] * bins[None, :] % samples
    return 2.0 * math.pi * phase.astype(jnp.float32) / samples


def forward_table(first, count, samples):
    angle = phase_angle(first, count, samples)
    return jnp.stack([jnp.cos(angle), -jnp.sin(angle)]).astype(jnp.bfloat16)


def inverse_table(count, samples):
    angle = jnp.transpose(phase_angle(0, count, samples))
    scale = 2.0 / samples
    return jnp.stack([scale * jnp.cos(angle), -scale * jnp.sin(angle)]).astype(jnp.bfloat16)


def body(response, focus_plus, onset):
    groups = lax.axis_size("freq")
    per_group = response.shape[1]
    nbin = per_group * groups
    samples = focus_plus.shape[1]
    first = lax.axis_index("freq") * per_group
    table = forward_table(first, per_group, samples)
    local = jnp.einsum(
        "xtr,ctj->cjxr",
        lax.all_gather(focus_plus, "freq", axis=0, tiled=True),
        table,
        preferred_element_type=jnp.float32,
    ).astype(jnp.bfloat16)
    piece = lax.all_gather(local, "src", axis=3, tiled=True)
    real_r = response[0]
    imag_r = response[1]
    real_f = piece[0]
    imag_f = piece[1]
    rr = jnp.einsum("bsr,bxr->bxs", real_r, real_f, preferred_element_type=jnp.float32)
    ii = jnp.einsum("bsr,bxr->bxs", imag_r, imag_f, preferred_element_type=jnp.float32)
    ri = jnp.einsum("bsr,bxr->bxs", real_r, imag_f, preferred_element_type=jnp.float32)
    ir = jnp.einsum("bsr,bxr->bxs", imag_r, real_f, preferred_element_type=jnp.float32)
    real_g = rr - ii
    imag_g = ri + ir
    convolved = jnp.stack([real_g, imag_g]).astype(jnp.bfloat16)
    inverse = inverse_table(nbin, samples)
    trace = jnp.einsum(
        "cjxs,cjt->xts",
        lax.all_to_all(convolved, "freq", split_axis=2, concat_axis=1, tiled=True),
        inverse,
        preferred_element_type=jnp.float32,
    )
    times = jnp.arange(samples, dtype=jnp.int32)
    keep = times[None, :, None] < onset[:, None, :]
    return jnp.where(keep, trace, 0.0).astype(jnp.bfloat16)


def solution(mesh):
    return jax.shard_map(
        body,
        mesh=mesh,
        in_specs=(P(None, "freq", "src", None), P("freq", None, "src"), P("freq", "src")),
        out_specs=P("freq", None, "src"),
        check_vma=False,
    )
```

profile of v0, /device:TPU:1, one launch (start us, length us, event | category | flops | bytes accessed | tf_op | source)
XLA Modules:
  0.0 328.4 jit_solution(12809570572432254139)
XLA Ops:
  6.5 0.0 all-gather.3.cloned.1.call-start
  6.5 0.7 all-gather.3.cloned.1.call-update
  7.3 0.0 all-gather.5.cloned.1.call-start
  7.3 0.1 cosine_convert_fusion
  7.5 160.9 %all-gather.3.cloned.1.call-done = bf16[192,256,256]{2,1,0:T(8,128)(2,1)} async-done(((bf16[12,256,256]{2,1,0:T(8,128)(2,1)}), bf16[192,256,256]{2,1,0:T(8,128)(2,1)}) %all-gather.3.cloned.1.call-update) | async-done | bytes 25165840 | tf_op jit(solution)/shard_map/all_gather | solution.py:36
  168.4 12.3 %fusion.19 = bf16[2,2,192,256]{3,1,2,0:T(2,128)(2,1)} fusion(bf16[192,256,256]{2,1,0:T(8,128)(2,1)} %all-gather.3.cloned.1.call-done, bf16[1,256,2]{1,2,0:T(2,128)(2,1)S(1)} %get-tuple-element.10, bf16[1,256,2]{1,2,0:T(2,128)(2,1)S(1)} %get-tuple-element.9), kind=kOutput, calls=%fused_computation.23 | convolution fusion | flops 100864000 | bytes 25561088 | tf_op jit(solution)/shard_map/xtr,ctj->cjxr/dot_general | solution.py:34
  180.6 0.0 all-gather.5.cloned.1.call-update
  180.7 94.0 %all-gather.5.cloned.1.call-done = bf16[2,2,192,4096]{3,1,2,0:T(2,128)(2,1)} async-done(((bf16[2,2,192,256]{3,1,2,0:T(2,128)(2,1)}), bf16[2,2,192,4096]{3,1,2,0:T(2,128)(2,1)}) %all-gather.5.cloned.1.call-update) | async-done | bytes 6291472 | tf_op jit(solution)/shard_map/all_gather | solution.py:40
  274.7 0.0 copy-start
  274.7 7.9 %slice_bitcast_fusion = (bf16[2,192,4096]{2,0,1:T(2,128)(2,1)S(1)}, bf16[2,192,4096]{2,0,1:T(2,128)(2,1)S(1)}) fusion(bf16[2,2,192,4096]{3,1,2,0:T(2,128)(2,1)} %all-gather.5.cloned.1.call-done), kind=kLoop, calls=%fused_computation.14 | loop fusion | bytes 12582912 | tf_op jit(solution)/shard_map/squeeze | solution.py:44
  282.7 0.0 copy-done
  282.7 2.3 fusion.4
  285.0 2.3 fusion.2
  287.3 2.3 fusion.42
  289.5 2.3 fusion.47
  291.8 0.0 copy-start.1
  291.9 1.2 copy.19
  293.1 16.1 %all-to-all-start = ((bf16[2,2,192,256]{3,1,0,2:T(2,128)(2,1)}), bf16[2,2,192,256]{3,1,0,2:T(2,128)(2,1)S(1)}, u32[]{:S(2)}, u32[]{:S(2)}) async-start(bf16[2,2,192,256]{3,1,0,2:T(2,128)(2,1)} %copy.19), calls=%async_computation | async-start | bytes 786432 | tf_op jit(solution)/shard_map/all_to_all | solution.py:55
  309.2 0.2 multiply_convert_fusion.1
  309.4 9.9 %all-to-all-done = bf16[2,2,192,256]{3,1,0,2:T(2,128)(2,1)S(1)} async-done(((bf16[2,2,192,256]{3,1,0,2:T(2,128)(2,1)}), bf16[2,2,192,256]{3,1,0,2:T(2,128)(2,1)S(1)}, u32[]{:S(2)}, u32[]{:S(2)}) %all-to-all-start) | async-done | bytes 393248 | tf_op jit(solution)/shard_map/all_to_all | solution.py:55
  319.2 0.4 copy.21
  319.6 0.2 all_to_all.16
  319.8 0.0 copy-done.1
  319.8 1.7 fusion.14
  (3 shorter events, 0.0 us)
Async XLA Ops:
  6.5 161.8 %all-gather.3.cloned.1.call-start = ((), (), s32[]{:S(2)}) async-start(), calls=%async_computation.1 | async-start | bytes 26738688 | tf_op jit(solution)/shard_map/all_gather | solution.py:36
  7.3 267.4 %all-gather.5.cloned.1.call-start = ((), (), s32[]{:S(2)}) async-start(), calls=%async_computation.2 | async-start | bytes 6684672 | tf_op jit(solution)/shard_map/all_gather | solution.py:40
  274.7 7.9 %copy-start = (bf16[2,2,256,4096]{3,2,1,0:T(8,128)(2,1)S(1)}, bf16[2,2,256,4096]{3,2,1,0:T(8,128)(2,1)}, u32[]{:S(2)}) copy-start(bf16[2,2,256,4096]{3,2,1,0:T(8,128)(2,1)} %param.3) | copy-start | bytes 25165828
  291.8 27.9 %copy-start.1 = (s32[12,256]{1,0:T(8,128)S(1)}, s32[12,256]{1,0:T(8,128)}, u32[]{:S(2)}) copy-start(s32[12,256]{1,0:T(8,128)} %param.5) | copy-start | bytes 36868
  293.1 26.2 %all-to-all-start = ((bf16[2,2,192,256]{3,1,0,2:T(2,128)(2,1)}), bf16[2,2,192,256]{3,1,0,2:T(2,128)(2,1)S(1)}, u32[]{:S(2)}, u32[]{:S(2)}) async-start(bf16[2,2,192,256]{3,1,0,2:T(2,128)(2,1)} %copy.19), calls=%async_computation | async-start | bytes 786432 | tf_op jit(solution)/shard_map/all_to_all | solution.py:55
Sparse Core Ops, SparseCore 0:
  10.1 158.2 all-gather.2
  180.8 93.8 all-gather.4
where the time goes:
time: 329 us; the launch traced here: 328 us
  waiting for transfers between devices  266 us (81%)
  matrix products  23.2 us (7%)
  starting transfers between devices  16.1 us (5%)
  between operations  13.5 us (4%)
  local copies, waits for them, and re-layouts  9.63 us (3%)
    all_gather x1, waiting for transfers between devices, body(): lax.all_gather(focus_plus, 'freq', axis=0, tiled=True)  161 us
    all_gather x1, waiting for transfers between devices, body(): piece = lax.all_gather(local, 'src', axis=3, tiled=True)  94 us
    all_to_all x1, starting transfers between devices, body(): lax.all_to_all(convolved, 'freq', split_axis=2, concat_axis=1, tiled=True)  16.1 us
    dot_general x1, matrix products, body(): jnp.einsum('xtr,ctj->cjxr', lax.all_gather(focus_plus, 'freq', axis=0, ti...  12.3 us
    all_to_all x1, waiting for transfers between devices, body(): lax.all_to_all(convolved, 'freq', split_axis=2, concat_axis=1, tiled=True)  9.86 us
    squeeze x1, local copies, waits for them, and re-layouts, body(): imag_f = piece[1]  7.94 us
  transfers between devices with their start and end apart: 3, of which 3 were waited for; matrix products, arithmetic and copies ran while one was open for 0% of the time, Pallas kernels for 0%

commit v1 on v0

--- a/solution.py
+++ b/solution.py
@@ -29,14 +29,11 @@
     per_group = response.shape[1]
     nbin = per_group * groups
     samples = focus_plus.shape[1]
-    first = lax.axis_index("freq") * per_group
-    table = forward_table(first, per_group, samples)
+    table = forward_table(0, nbin, samples)
     local = jnp.einsum(
-        "xtr,ctj->cjxr",
-        lax.all_gather(focus_plus, "freq", axis=0, tiled=True),
-        table,
-        preferred_element_type=jnp.float32,
+        "xtr,ctj->cjxr", focus_plus, table, preferred_element_type=jnp.float32
     ).astype(jnp.bfloat16)
+    local = lax.all_to_all(local, "freq", split_axis=1, concat_axis=2, tiled=True)
     piece = lax.all_gather(local, "src", axis=3, tiled=True)
     real_r = response[0]
     imag_r = response[1]

time: 329 us -> 173 us (0.53)
  waiting for transfers between devices: 266 us -> 105 us
  blocking collectives: 0 us -> 18.3 us
  matrix products: 23.2 us -> 13.6 us
  local copies, waits for them, and re-layouts: 9.63 us -> 5.08 us
    all_gather x1 -> x0, waiting for transfers between devices: 161 us -> none  [body(): lax.all_gather(focus_plus, 'freq', axis=0, tiled=True)]
    all_to_all x0 -> x1, blocking collectives: none -> 18.3 us  [body(): lax.all_to_all(local, 'freq', split_axis=1, concat_axis=2, tiled=True)]
    dot_general x1, matrix products: 12.3 us -> 0.39 us  [body(): jnp.einsum('xtr,ctj->cjxr', focus_plus, table, preferred_element_type=jnp...]
    squeeze x1 -> x0, local copies, waits for them, and re-layouts: 7.94 us -> none  [body(): imag_f = piece[1]]
  transfers between devices with their start and end apart: 3 -> 2, of which waited for: 3 -> 2; matrix products, arithmetic and copies ran while one was open for 0% -> 0% of each run, Pallas kernels for 0% -> 0%
where the time goes in v1:
time: 173 us; the launch traced here: 172 us
  waiting for transfers between devices  105 us (61%)
  blocking collectives  18.3 us (11%)
  starting transfers between devices  16.1 us (9%)
  matrix products  13.6 us (8%)
  between operations  13.5 us (8%)
  local copies, waits for them, and re-layouts  5.08 us (3%)
    all_gather x1, waiting for transfers between devices, body(): piece = lax.all_gather(local, 'src', axis=3, tiled=True)  95.5 us
    all_to_all x1, blocking collectives, body(): lax.all_to_all(local, 'freq', split_axis=1, concat_axis=2, tiled=True)  18.3 us
    all_to_all x1, starting transfers between devices, body(): lax.all_to_all(convolved, 'freq', split_axis=2, concat_axis=1, tiled=True)  16.1 us
    all_to_all x1, waiting for transfers between devices, body(): lax.all_to_all(convolved, 'freq', split_axis=2, concat_axis=1, tiled=True)  9.87 us
    dot_general x1, matrix products, body(): jnp.einsum('bsr,bxr->bxs', imag_r, imag_f, preferred_element_type=jnp.flo...  4.81 us
    dot_general x1, matrix products, body(): jnp.einsum('bsr,bxr->bxs', imag_r, real_f, preferred_element_type=jnp.flo...  3.6 us
  transfers between devices with their start and end apart: 2, of which 2 were waited for; matrix products, arithmetic and copies ran while one was open for 0% of the time, Pallas kernels for 0%

profile of v1, /device:TPU:1, one launch (start us, length us, event | category | flops | bytes accessed | tf_op | source)
XLA Modules:
  0.0 172.5 jit_solution(12629588674767020763)
XLA Ops:
  6.5 0.0 copy-start
  6.5 0.0 all-gather.2.cloned.1.call-start
  6.5 0.2 cosine_convert_fusion
  6.8 1.2 copy-done
  7.9 0.4 fusion.15
  8.3 0.4 copy.16
  8.8 18.3 %all_to_all.36 = bf16[2,32,12,256]{3,0,2,1:T(2,128)(2,1)S(1)} all-to-all(bf16[2,32,12,256]{3,0,2,1:T(2,128)(2,1)S(1)} %copy.16), channel_id=1, replica_groups=mesh['freq'=16,'src'=16] {'freq'}, dimensions={1} | all-to-all | bytes 786432 | tf_op jit(solution)/shard_map/all_to_all | solution.py:36
  27.1 0.3 copy.17
  27.4 0.8 copy.18
  28.2 0.0 all-gather.2.cloned.1.call-update
  28.2 95.5 %all-gather.2.cloned.1.call-done = bf16[2,2,192,4096]{3,2,1,0:T(8,128)(2,1)} async-done(((bf16[2,2,192,256]{3,2,1,0:T(8,128)(2,1)}), bf16[2,2,192,4096]{3,2,1,0:T(8,128)(2,1)}) %all-gather.2.cloned.1.call-update) | async-done | bytes 6291472 | tf_op jit(solution)/shard_map/all_gather | solution.py:37
  123.7 0.0 copy-start.1
  123.7 0.0 slice-start
  123.7 4.8 %fusion.2 = f32[2,192,256]{2,1,0:T(8,128)S(1)} fusion(bf16[2,2,256,4096]{3,2,1,0:T(8,128)(2,1)} %param.3, bf16[2,2,192,4096]{3,2,1,0:T(8,128)(2,1)} %all-gather.2.cloned.1.call-done), kind=kOutput, calls=%fused_computation.2 | convolution fusion | flops 805306368 | bytes 7733248 | tf_op jit(solution)/shard_map/bsr,bxr->bxs/dot_general | solution.py:43
  128.5 0.7 copy-done.1
  129.2 0.0 slice-start.1
  129.2 3.6 %fusion = f32[2,192,256]{2,1,0:T(8,128)S(1)} fusion(bf16[2,2,256,4096]{3,2,1,0:T(8,128)(2,1)S(1)} %copy-done.1, bf16[2,2,192,4096]{3,2,1,0:T(8,128)(2,1)} %all-gather.2.cloned.1.call-done), kind=kOutput, calls=%fused_computation | convolution fusion | flops 805306368 | bytes 7733248 | tf_op jit(solution)/shard_map/bsr,bxr->bxs/dot_general | solution.py:45
  132.8 0.0 slice-done
  132.8 0.0 slice-done.1
  132.9 1.5 fusion.30
  134.4 0.0 copy-start.2
  134.4 1.5 fusion.33
  136.0 1.2 copy.19
  137.1 16.1 %all-to-all-start.1 = ((bf16[2,2,192,256]{3,1,0,2:T(2,128)(2,1)}), bf16[2,2,192,256]{3,1,0,2:T(2,128)(2,1)S(1)}, u32[]{:S(2)}, u32[]{:S(2)}) async-start(bf16[2,2,192,256]{3,1,0,2:T(2,128)(2,1)} %copy.19), calls=%async_computation.1 | async-start | bytes 786432 | tf_op jit(solution)/shard_map/all_to_all | solution.py:52
  153.2 0.2 multiply_convert_fusion.1
  153.5 9.9 %all-to-all-done.1 = bf16[2,2,192,256]{3,1,0,2:T(2,128)(2,1)S(1)} async-done(((bf16[2,2,192,256]{3,1,0,2:T(2,128)(2,1)}), bf16[2,2,192,256]{3,1,0,2:T(2,128)(2,1)S(1)}, u32[]{:S(2)}, u32[]{:S(2)}) %all-to-all-start.1) | async-done | bytes 393248 | tf_op jit(solution)/shard_map/all_to_all | solution.py:52
  163.3 0.4 copy.21
  163.7 0.2 all_to_all.33
  163.9 0.0 copy-done.2
  163.9 1.7 %fusion.12 = bf16[12,256,256]{2,1,0:T(8,128)(2,1)} fusion(bf16[2,32,12,256]{3,1,0,2:T(8,128)(2,1)S(1)} %all_to_all.33, s32[12,256]{1,0:T(8,128)S(1)} %copy-done.2, bf16[1,32,256]{2,1,0:T(8,128)(2,1)S(1)} %get-tuple-element.6, bf16[1,32,256]{2,1,0:T(8,128)(2,1)S(1)} %get-tuple-element.5), kind=kOutput, calls=%fused_computation.15 | convolution fusion | flops 103088128 | bytes 2011136 | tf_op jit(solution)/shard_map/cjxs,cjt->xts/dot_general | solution.py:50
  (3 shorter events, 0.0 us)
Async XLA Ops:
  6.5 1.4 copy-start
  6.5 117.2 %all-gather.2.cloned.1.call-start = ((), (), s32[]{:S(2)}) async-start(), calls=%async_computation.2 | async-start | bytes 6684672 | tf_op jit(solution)/shard_map/all_gather | solution.py:37
  123.7 5.5 %copy-start.1 = (bf16[2,2,256,4096]{3,2,1,0:T(8,128)(2,1)S(1)}, bf16[2,2,256,4096]{3,2,1,0:T(8,128)(2,1)}, u32[]{:S(2)}) copy-start(bf16[2,2,256,4096]{3,2,1,0:T(8,128)(2,1)} %param.3) | copy-start | bytes 25165828
  123.7 9.1 %slice-start = ((s8[6291456]{0:T(1024)(128)(4,1)}), s8[4194304]{0:T(1024)(128)(4,1)S(1)}, s32[]{:S(2)}) async-start(s8[6291456]{0:T(1024)(128)(4,1)} %bitcast.79), calls=%async_computation.3 | async-start | bytes 8388608
  129.2 3.6 %slice-start.1 = ((s8[6291456]{0:T(1024)(128)(4,1)}), s8[2097152]{0:T(1024)(128)(4,1)S(1)}, s32[]{:S(2)}) async-start(s8[6291456]{0:T(1024)(128)(4,1)} %bitcast.79), calls=%async_computation.4 | async-start | bytes 4194304
  134.4 29.5 %copy-start.2 = (s32[12,256]{1,0:T(8,128)S(1)}, s32[12,256]{1,0:T(8,128)}, u32[]{:S(2)}) copy-start(s32[12,256]{1,0:T(8,128)} %param.5) | copy-start | bytes 36868
  137.1 26.2 %all-to-all-start.1 = ((bf16[2,2,192,256]{3,1,0,2:T(2,128)(2,1)}), bf16[2,2,192,256]{3,1,0,2:T(2,128)(2,1)S(1)}, u32[]{:S(2)}, u32[]{:S(2)}) async-start(bf16[2,2,192,256]{3,1,0,2:T(2,128)(2,1)} %copy.19), calls=%async_computation.1 | async-start | bytes 786432 | tf_op jit(solution)/shard_map/all_to_all | solution.py:52
Sparse Core Ops, SparseCore 0:
  28.3 95.3 all-gather.1

commit v2 on v1

v2 whole, which is shorter than its diff:
```python
import math

import jax
import jax.numpy as jnp
import ml_dtypes
import numpy as np
from jax import lax
from jax.experimental import pallas as pl
from jax.experimental.pallas import tpu as pltpu
from jax.sharding import PartitionSpec as P

MESH = pl.DeviceIdType.MESH

NX = 4
NH = 2
NZ = 8
CHIPS = NX * NH
NJ = 2
FOCAL = 12
PAIR = 2 * FOCAL
BLOCK = 2 * PAIR
ROWS = CHIPS * BLOCK
HALF = CHIPS * NJ * 2
NT = 256
LANES = 128
WIDTH = 256
PLACES = ((0, 0), (1, 0), (3, 0), (0, 1), (2, 0), (1, 1), (3, 1), (2, 1))
ROWS_A = 3 * BLOCK


def tables():
    samples = np.arange(NT, dtype=np.int32)
    core, owner, chip, bins, part = np.meshgrid(
        np.arange(2), np.arange(2), np.arange(CHIPS), np.arange(NJ), np.arange(2), indexing="ij"
    )
    index = 4 * chip + 2 * (core ^ owner) + bins + 1
    index = index.reshape(2, 2 * HALF)
    part = part.reshape(2, 2 * HALF)
    phase = (index[..., None] * samples) % NT
    angle = (np.float32(2.0 * math.pi) * phase.astype(np.float32) / np.float32(NT)).astype(np.float32)
    wave = np.where(part[..., None] == 0, np.cos(angle), -np.sin(angle)).astype(np.float32)
    forward = wave.astype(ml_dtypes.bfloat16)
    inverse = (np.float32(2.0 / NT) * wave).astype(ml_dtypes.bfloat16)
    return forward, np.ascontiguousarray(inverse.transpose(0, 2, 1))


def gather_kernel(
    resp_hbm, focus_hbm, table_ref, out_ref,
    resp, focus, mine, pair_out, pair_in, blocks, gath, acc, back_out, back_in, last_out, last_in,
    load_sem, pair_s, pair_r, fwd_s, fwd_r, a_s, a_r, z_s, z_r, y_s, y_r, inv_s, inv_r, last_s, last_r,
):
    f = lax.axis_index("freq")
    me = lax.axis_index("src")
    core = f % 2
    yh = (f // 2) % 2
    x = f // 4
    chip = f // 2
    y = me // NZ
    z = me % NZ
    sibling = (f + 1 - 2 * core, me)
    partner = (1 - y) * NZ + z
    up = (f, y * NZ + (z + 1) % NZ)
    down = (f, y * NZ + (z + NZ - 1) % NZ)
    across = (f, partner)

    def chip_at(dx, dy):
        return ((x + dx) % NX) * NH + (yh + dy) % NH

    ahead = [chip_at(dx, dy) for dx, dy in PLACES]
    behind = [chip_at(NX - dx, dy) for dx, dy in PLACES]

    load_focus = pltpu.make_async_copy(focus_hbm, focus, load_sem.at[0])
    load_focus.start()
    barrier = pltpu.get_barrier_semaphore()
    for peer in [sibling, up, down, across] + [(2 * c + core, me) for c in ahead[1:]]:
        pl.semaphore_signal(barrier, inc=1, device_id=peer, device_id_type=MESH)
    load_focus.wait()
    load_resp = pltpu.make_async_copy(resp_hbm, resp, load_sem.at[1])
    load_resp.start()

    def put(i, rows):
        for h in range(2):
            mine[h, pl.ds(i, HALF, stride=PAIR), :] = rows[:, h * LANES : (h + 1) * LANES]

    def take(i):
        halves = [mine[h, pl.ds(i, HALF, stride=PAIR), :] for h in range(2)]
        return jnp.concatenate(halves, axis=1).astype(jnp.bfloat16)

    def transform(i, _):
        res = jnp.dot(table_ref[core], focus[i], preferred_element_type=jnp.float32)
        put(core * FOCAL + i, res[:HALF])
        pair_out[i] = res[HALF:].astype(jnp.bfloat16)
        return 0

    lax.fori_loop(0, FOCAL, transform, 0)
    acc[...] = jnp.zeros_like(acc)
    pl.semaphore_wait(barrier, 4 + len(PLACES) - 1)
    swap = pltpu.make_async_remote_copy(
        src_ref=pair_out, dst_ref=pair_in, send_sem=pair_s.at[0], recv_sem=pair_r.at[0],
        device_id=sibling, device_id_type=MESH,
    )
    swap.start()
    swap.wait_recv()

    def place(i, _):
        put((1 - core) * FOCAL + i, pair_in[i].astype(jnp.float32))
        return 0

    lax.fori_loop(0, FOCAL, place, 0)
    for h in range(2):
        blocks[:, :, :, pl.ds(h * LANES, LANES)] = mine[h].astype(jnp.bfloat16).reshape(CHIPS, NJ, BLOCK, LANES)

    def forward_copy(p):
        rows = pl.ds(p * BLOCK, BLOCK)
        return pltpu.make_async_remote_copy(
            src_ref=blocks.at[behind[p]], dst_ref=gath.at[:, me, rows],
            send_sem=fwd_s.at[p], recv_sem=fwd_r.at[p],
            device_id=(2 * behind[p] + core, me), device_id_type=MESH,
        )

    for p in range(1, len(PLACES)):
        forward_copy(p).start()
    gath[:, me, :BLOCK, :] = blocks[chip]

    part_a = (0, ROWS_A)
    part_b = (ROWS_A, ROWS - ROWS_A)
    spans = (part_b, part_a, part_a)
    rings = (up, down)

    def z_copy(d, t, s, o):
        block = gath.at[d, o, pl.ds(*spans[t])]
        return pltpu.make_async_remote_copy(
            src_ref=block, dst_ref=block, send_sem=z_s.at[d, t, s], recv_sem=z_r.at[d, t, s],
            device_id=rings[d], device_id_type=MESH,
        )

    def y_copy(d, s, o):
        block = gath.at[d, o, pl.ds(*part_b)]
        return pltpu.make_async_remote_copy(
            src_ref=block, dst_ref=block, send_sem=y_s.at[d, s], recv_sem=y_r.at[d, s],
            device_id=across, device_id_type=MESH,
        )

    def a_copy(o):
        block = gath.at[:, o, pl.ds(*part_a)]
        return pltpu.make_async_remote_copy(
            src_ref=block, dst_ref=block, send_sem=a_s.at[0], recv_sem=a_r.at[0],
            device_id=across, device_id_type=MESH,
        )

    def products(d, o, span):
        rows = pl.ds(*span)
        piece = gath[d, o, rows, :]
        columns = pl.ds(pl.multiple_of(o * WIDTH, WIDTH), WIDTH)
        for c in range(2):
            acc[d, c, rows, :] += lax.dot_general(
                piece, resp[c, d, :, columns], (((1,), (1,)), ((), ())),
                preferred_element_type=jnp.float32,
            )

    def at(d, s):
        return (z + NZ - s) % NZ if d == 0 else (z + s) % NZ

    for p in (1, 2):
        forward_copy(p).wait_recv()
    a_copy(me).start()
    for d in range(NJ):
        z_copy(d, 1, 0, me).start()
    for p in range(3, len(PLACES)):
        forward_copy(p).wait_recv()
    for d in range(NJ):
        z_copy(d, 0, 0, me).start()
        y_copy(d, 0, me).start()
    load_resp.wait()
    for d in range(NJ):
        products(d, me, part_a)
    a_copy(partner).wait_recv()
    for d in range(NJ):
        z_copy(d, 2, 0, partner).start()
    for d in range(NJ):
        products(d, me, part_b)
        products(d, partner, part_a)

    def step(s, _):
        for t in range(3):
            for d in range(NJ):
                o = (y if t < 2 else 1 - y) * NZ + at(d, s + 1)
                z_copy(d, t, s, o).wait_recv()

                @pl.when(s < NZ - 2)
                def _():
                    z_copy(d, t, s + 1, o).start()

                if t == 0:
                    y_copy(d, s + 1, o).start()
                products(d, o, spans[t])
        for d in range(NJ):
            o = (1 - y) * NZ + at(d, s)
            y_copy(d, s, o).wait_recv()
            products(d, o, part_b)
        return 0

    lax.fori_loop(0, NZ - 1, step, 0)
    for d in range(NJ):
        o = (1 - y) * NZ + at(d, NZ - 1)
        y_copy(d, NZ - 1, o).wait_recv()
        products(d, o, part_b)

    def back_copy(p):
        return pltpu.make_async_remote_copy(
            src_ref=back_out.at[p], dst_ref=back_in.at[chip],
            send_sem=inv_s.at[p], recv_sem=inv_r.at[p],
            device_id=(2 * ahead[p] + core, me), device_id_type=MESH,
        )

    for p in range(len(PLACES) - 1, -1, -1):
        for d in range(NJ):
            start = p * BLOCK
            re = acc[d, 0, start : start + PAIR, :] - acc[d, 1, start + PAIR : start + BLOCK, :]
            im = acc[d, 0, start + PAIR : start + BLOCK, :] + acc[d, 1, start : start + PAIR, :]
            both = jnp.concatenate([re, im], axis=0).astype(jnp.bfloat16)
            if p == 0:
                back_in[chip, d] = both
            else:
                back_out[p, d] = both
        if p > 0:
            back_copy(p).start()
    for p in range(1, len(PLACES)):
        back_copy(p).wait_recv()
    for h in range(2):
        mine[h] = back_in[:, :, :, pl.ds(h * LANES, LANES)].astype(jnp.float32).reshape(HALF * PAIR, LANES)

    def theirs(i, _):
        last_out[i] = take((1 - core) * FOCAL + i)
        return 0

    lax.fori_loop(0, FOCAL, theirs, 0)
    last = pltpu.make_async_remote_copy(
        src_ref=last_out, dst_ref=last_in, send_sem=last_s.at[0], recv_sem=last_r.at[0],
        device_id=sibling, device_id_type=MESH,
    )
    last.start()

    def own(i, _):
        out_ref[i, :HALF, :] = take(core * FOCAL + i)
        return 0

    lax.fori_loop(0, FOCAL, own, 0)
    last.wait_recv()
    out_ref[:, HALF:, :] = last_in[...]

    last.wait_send()
    swap.wait_send()
    a_copy(me).wait_send()
    for p in range(1, len(PLACES)):
        forward_copy(p).wait_send()
        back_copy(p).wait_send()

    def drain(s, _):
        for d in range(NJ):
            for t in range(3):
                z_copy(d, t, s, me).wait_send()
            y_copy(d, s, me).wait_send()
        return 0

    lax.fori_loop(0, NZ - 1, drain, 0)
    for d in range(NJ):
        y_copy(d, NZ - 1, me).wait_send()


def gather(response, focus_plus, table):
    bf16 = jnp.bfloat16
    dma = pltpu.SemaphoreType.DMA
    places = len(PLACES)
    return pl.pallas_call(
        gather_kernel,
        out_shape=jax.ShapeDtypeStruct((FOCAL, 2 * HALF, WIDTH), bf16),
        in_specs=[
            pl.BlockSpec(memory_space=pl.ANY),
            pl.BlockSpec(memory_space=pl.ANY),
            pl.BlockSpec(memory_space=pltpu.VMEM),
        ],
        out_specs=pl.BlockSpec(memory_space=pltpu.VMEM),
        scratch_shapes=[
            pltpu.VMEM(response.shape, bf16),
            pltpu.VMEM(focus_plus.shape, bf16),
            pltpu.VMEM((2, HALF * PAIR, LANES), jnp.float32),
            pltpu.VMEM((FOCAL, HALF, WIDTH), bf16),
            pltpu.VMEM((FOCAL, HALF, WIDTH), bf16),
            pltpu.VMEM((CHIPS, NJ, BLOCK, WIDTH), bf16),
            pltpu.VMEM((NJ, 2 * NZ, ROWS, WIDTH), bf16),
            pltpu.VMEM((NJ, 2, ROWS, WIDTH), jnp.float32),
            pltpu.VMEM((CHIPS, NJ, BLOCK, WIDTH), bf16),
            pltpu.VMEM((CHIPS, NJ, BLOCK, WIDTH), bf16),
            pltpu.VMEM((FOCAL, HALF, WIDTH), bf16),
            pltpu.VMEM((FOCAL, HALF, WIDTH), bf16),
            dma((2,)),
            dma((1,)), dma((1,)),
            dma((places,)), dma((places,)),
            dma((1,)), dma((1,)),
            dma((NJ, 3, NZ - 1)), dma((NJ, 3, NZ - 1)),
            dma((NJ, NZ)), dma((NJ, NZ)),
            dma((places,)), dma((places,)),
            dma((1,)), dma((1,)),
        ],
        compiler_params=pltpu.CompilerParams(
            collective_id=0, has_side_effects=True, vmem_limit_bytes=40 << 20
        ),
        name="gather",
    )(response, focus_plus, table)


GROUP = 3


def inverse_kernel(spectra_ref, table_ref, onset_ref, out_ref):
    core = lax.axis_index("freq") % 2
    table = table_ref[core]
    times = lax.broadcasted_iota(jnp.int32, (NT, WIDTH), 0)
    first = pl.program_id(0) * GROUP
    for i in range(GROUP):
        trace = jnp.dot(table, spectra_ref[i], preferred_element_type=jnp.float32)
        onset = onset_ref[pl.ds(first + i, 1), :]
        out_ref[i] = jnp.where(times < onset, trace, 0.0).astype(jnp.bfloat16)


def inverse(spectra, table, onset):
    return pl.pallas_call(
        inverse_kernel,
        grid=(FOCAL // GROUP,),
        out_shape=jax.ShapeDtypeStruct((FOCAL, NT, WIDTH), jnp.bfloat16),
        in_specs=[
            pl.BlockSpec((GROUP, 2 * HALF, WIDTH), lambda i: (i, 0, 0)),
            pl.BlockSpec((2, NT, 2 * HALF), lambda i: (0, 0, 0)),
            pl.BlockSpec((FOCAL, WIDTH), lambda i: (0, 0)),
        ],
        out_specs=pl.BlockSpec((GROUP, NT, WIDTH), lambda i: (i, 0, 0)),
        name="inverse",
    )(spectra, table, onset)


def body(response, focus_plus, onset):
    forward_table, inverse_table = tables()
    spectra = gather(response, focus_plus, jnp.asarray(forward_table))
    return inverse(spectra, jnp.asarray(inverse_table), onset)


def solution(mesh):
    return jax.shard_map(
        body,
        mesh=mesh,
        in_specs=(P(None, "freq", "src", None), P("freq", None, "src"), P("freq", "src")),
        out_specs=P("freq", None, "src"),
        check_vma=False,
    )
```

time: 173 us -> 87 us (0.50)
  waiting for transfers between devices: 105 us -> 0 us
  Pallas kernels: 0 us -> 80.4 us
  blocking collectives: 18.3 us -> 0 us
  starting transfers between devices: 16.1 us -> 0 us
  matrix products: 13.6 us -> 0 us
  between operations: 13.5 us -> 0.02 us
    all_gather x1 -> x0, waiting for transfers between devices: 95.5 us -> none  [body(): piece = lax.all_gather(local, 'src', axis=3, tiled=True)]
    pallas_call x0 -> x2, Pallas kernels: none -> 80.4 us  [the longest x1 76.5 us: gather(): pl.pallas_call(gather_kernel, out_shape=jax.ShapeDtypeStruct((FOCAL, 2 *...]
    all_to_all x1 -> x0, blocking collectives: 18.3 us -> none  [body(): lax.all_to_all(local, 'freq', split_axis=1, concat_axis=2, tiled=True)]
    all_to_all x1 -> x0, starting transfers between devices: 16.1 us -> none  [body(): lax.all_to_all(convolved, 'freq', split_axis=2, concat_axis=1, tiled=True)]
    dot_general x6 -> x0, matrix products: 13.6 us -> none  [the longest x1 4.81 us: body(): jnp.einsum('bsr,bxr->bxs', imag_r, imag_f, preferred_element_type=jnp.flo...]
    all_to_all x1 -> x0, waiting for transfers between devices: 9.87 us -> none  [body(): lax.all_to_all(convolved, 'freq', split_axis=2, concat_axis=1, tiled=True)]
    unnamed x10 -> x8, local copies, waits for them, and re-layouts: 1.9 us -> 6.37 us
  transfers between devices with their start and end apart: 2 -> 0, of which waited for: 2 -> 0; matrix products, arithmetic and copies ran while one was open for 0% -> 0% of each run, Pallas kernels for 0% -> 0%
where the time goes in v2:
time: 87 us; the launch traced here: 86.8 us
  Pallas kernels  80.4 us (92%)
  local copies, waits for them, and re-layouts  6.37 us (7%)
    pallas_call x1, Pallas kernels, gather(): pl.pallas_call(gather_kernel, out_shape=jax.ShapeDtypeStruct((FOCAL, 2 *...  76.5 us
    unnamed x8, local copies, waits for them, and re-layouts  6.37 us
    pallas_call x1, Pallas kernels, inverse(): pl.pallas_call(inverse_kernel, grid=(FOCAL // GROUP,), out_shape=jax.Shap...  3.83 us

profile of v2, /device:TPU:1, one launch (start us, length us, event | category | flops | bytes accessed | tf_op | source)
XLA Modules:
  0.0 86.8 jit_solution(6414806061012701530)
XLA Ops:
  0.0 0.0 copy-start
  0.0 3.4 %copy-done = bf16[2,2,256,4096]{3,2,1,0:T(8,128)(2,1)S(1)} copy-done((bf16[2,2,256,4096]{3,2,1,0:T(8,128)(2,1)S(1)}, bf16[2,2,256,4096]{3,2,1,0:T(8,128)(2,1)}, u32[]{:S(2)}) %copy-start) | copy-done | bytes 8388632
  3.4 0.0 copy-start.2
  3.4 1.4 %copy-done.2 = bf16[12,256,256]{2,1,0:T(8,128)(2,1)S(1)} copy-done((bf16[12,256,256]{2,1,0:T(8,128)(2,1)S(1)}, bf16[12,256,256]{2,1,0:T(8,128)(2,1)}, u32[]{:S(2)}) %copy-start.2) | copy-done | bytes 1572888
  4.8 0.0 copy-start.3
  4.8 0.8 copy-done.3
  5.6 76.5 %gather.1.spectra_ref = bf16[12,64,256]{2,1,0:T(8,128)(2,1)S(1)} custom-call(bf16[2,2,256,4096]{3,2,1,0:T(8,128)(2,1)S(1)} %copy-done, bf16[12,256,256]{2,1,0:T(8,128)(2,1)S(1)} %copy-done.2, bf16[2,64,256]{2,1,0:T(8,128)(2,1)S(1)} %copy-done.3), custom_call_target="tpu_custom_call" | custom-call | tf_op jit(solution)/shard_map/gather/pallas_call | solution.py:275
  82.2 0.0 copy-start.1
  82.2 0.7 copy-done.1
  82.9 3.8 %inverse.1 = bf16[12,256,256]{2,1,0:T(8,128)(2,1)} custom-call(bf16[12,64,256]{2,1,0:T(8,128)(2,1)} %copy-done.1, bf16[2,256,64]{2,1,0:T(8,128)(2,1)} %constant.5.clone.table_ref, s32[12,256]{1,0:T(8,128)} %onset_ref.1), custom_call_target="tpu_custom_call" | custom-call | tf_op jit(solution)/shard_map/inverse/pallas_call | solution.py:328
Async XLA Ops:
  0.0 3.4 %copy-start = (bf16[2,2,256,4096]{3,2,1,0:T(8,128)(2,1)S(1)}, bf16[2,2,256,4096]{3,2,1,0:T(8,128)(2,1)}, u32[]{:S(2)}) copy-start(bf16[2,2,256,4096]{3,2,1,0:T(8,128)(2,1)} %resp_hbm.1) | copy-start | bytes 25165828
  3.4 1.4 %copy-start.2 = (bf16[12,256,256]{2,1,0:T(8,128)(2,1)S(1)}, bf16[12,256,256]{2,1,0:T(8,128)(2,1)}, u32[]{:S(2)}) copy-start(bf16[12,256,256]{2,1,0:T(8,128)(2,1)} %focus_hbm.1) | copy-start | bytes 4718596
  4.8 0.8 copy-start.3
  82.2 0.8 copy-start.1

commit v3 on v1

v3 whole, which is shorter than its diff:
```python
import functools
import math

import jax
import jax.numpy as jnp
import ml_dtypes
import numpy as np
from jax import lax
from jax.experimental import pallas as pl
from jax.experimental.pallas import tpu as pltpu
from jax.sharding import PartitionSpec as P

MESH = pl.DeviceIdType.MESH

NX = 4
NH = 2
NZ = 8
CHIPS = NX * NH
PEERS = 2 * CHIPS
NJ = 2
FOCAL = 12
GROUPS = 3
FEW = FOCAL // GROUPS
TILE = NJ * 2 * FEW
PIECE = 2 * FEW
ROWS = PEERS * PIECE
HALF = NJ * 2 * PEERS
NT = 256
LANES = 128
WIDTH = 256
FAR = NZ // 2
CHIP_PLACES = ((0, 0), (1, 0), (3, 0), (0, 1), (2, 0), (1, 1), (3, 1), (2, 1))
PLACES = tuple((dx, dy, dc) for dx, dy in CHIP_PLACES for dc in range(2))
BATCHES = ((0, 1), (1, 1), (2, 1))
PLACES_A = (3, 3, 4)
STARTS = (0.0, 0.2, 0.4)
LEADS = (1.5, 0.5)
LAG = 1.05


def tables():
    samples = np.arange(NT, dtype=np.int32)
    bins = (np.arange(HALF) // 2 + 1).astype(np.int32)
    part = np.arange(HALF) % 2
    phase = (bins[:, None] * samples) % NT
    angle = (np.float32(2.0 * math.pi) * phase.astype(np.float32) / np.float32(NT)).astype(np.float32)
    wave = np.where(part[:, None] == 0, np.cos(angle), -np.sin(angle)).astype(np.float32)
    inverse = np.float32(2.0 / NT) * wave
    return wave.astype(ml_dtypes.bfloat16), np.ascontiguousarray(inverse.T).astype(ml_dtypes.bfloat16)


def gather_kernel(
    resp_hbm, focus_hbm, table_hbm, out_hbm,
    resp, focus, table, mine, blocks, arrived, gath, acc, back_out,
    load_sem, own_sem, fwd_s, fwd_r, a_s, a_r, z_s, z_r, y_s, y_r, inv_s, inv_r,
):
    f = lax.axis_index("freq")
    me = lax.axis_index("src")
    core = f % 2
    yh = (f // 2) % 2
    x = f // 4
    y = me // NZ
    z = me % NZ
    partner = (1 - y) * NZ + z
    rings = ((f, y * NZ + (z + 1) % NZ), (f, y * NZ + (z + NZ - 1) % NZ))
    across = (f, partner)

    def device_at(dx, dy, dc):
        return (((x + dx) % NX) * NH + (yh + dy) % NH) * 2 + (core + dc) % 2

    ahead = [device_at(*place) for place in PLACES]
    behind = [device_at(NX - dx, dy, dc) for dx, dy, dc in PLACES]
    batches = range(len(BATCHES))

    def few(ref, g):
        return ref.at[pl.ds(g * FEW, FEW)]

    def load_focus(g):
        return pltpu.make_async_copy(few(focus_hbm, g), few(focus, g), load_sem.at[g])

    load_table = pltpu.make_async_copy(table_hbm, table, load_sem.at[GROUPS])
    load_resp = pltpu.make_async_copy(resp_hbm, resp, load_sem.at[GROUPS + 1])
    load_table.start()
    for g in range(GROUPS):
        load_focus(g).start()
    barrier = pltpu.get_barrier_semaphore()
    peers = [*rings, across] + [(d, me) for d in ahead[1:]]
    for peer in peers:
        pl.semaphore_signal(barrier, inc=1, device_id=peer, device_id_type=MESH)

    def transform(g):
        load_focus(g).wait()
        waves = table[...]

        def one(i, _):
            res = jnp.dot(waves, focus[g * FEW + i], preferred_element_type=jnp.float32)
            for h in range(2):
                mine[g, h, pl.ds(i, HALF, stride=FEW), :] = res[:, h * LANES : (h + 1) * LANES]
            return 0

        lax.fori_loop(0, FEW, one, 0)
        for h in range(2):
            rows = mine[g, h].astype(jnp.bfloat16).reshape(PEERS, TILE, LANES)
            blocks[g, :, :, pl.ds(h * LANES, LANES)] = rows

    def groups_of(b):
        return pl.ds(*BATCHES[b])

    def forward_copy(b, q):
        return pltpu.make_async_remote_copy(
            src_ref=blocks.at[groups_of(b), behind[q]], dst_ref=arrived.at[groups_of(b), q],
            send_sem=fwd_s.at[b, q], recv_sem=fwd_r.at[b, q],
            device_id=(behind[q], me), device_id_type=MESH,
        )

    def spread(b):
        for q in range(1, PEERS):
            forward_copy(b, q).start()
        first, count = BATCHES[b]
        for g in range(first, first + count):
            arrived[g, 0] = blocks[g, f]

    def collect(b, first_chip, last_chip):
        for q in range(max(1, 2 * first_chip), 2 * last_chip):
            forward_copy(b, q).wait_recv()
        first, count = BATCHES[b]
        for g in range(first, first + count):
            for p in range(first_chip, last_chip):
                both = [arrived[g, 2 * p + c].astype(jnp.float32) for c in range(2)]
                for j in range(NJ):
                    rows = [tile[j * PIECE : (j + 1) * PIECE] for tile in both]
                    gath[j, me, g, p] = jnp.concatenate(rows, axis=0).astype(jnp.bfloat16)

    def span(b, t):
        return pl.ds(0, PLACES_A[b]) if t else pl.ds(PLACES_A[b], CHIPS - PLACES_A[b])

    def owner(d, r, column):
        return column * NZ + ((z + 2 * NZ - 1 - r) % NZ if d == 0 else (z + 1 + r) % NZ)

    def piece(b, d, r, o, places):
        if r < FAR - 1:
            return gath.at[:, o, groups_of(b), places]
        return gath.at[d, o, groups_of(b), places]

    def z_copy(d, t, b, r, o):
        block = piece(b, d, r, o, span(b, t))
        return pltpu.make_async_remote_copy(
            src_ref=block, dst_ref=block, send_sem=z_s.at[d, t, b, r], recv_sem=z_r.at[d, t, b, r],
            device_id=rings[d], device_id_type=MESH,
        )

    def z_send(d, t, b, r):
        return z_copy(d, t, b, r, owner(d, r - 1, 1 - y if t == 2 else y))

    def z_recv(d, t, b, r):
        return z_copy(d, t, b, r, owner(d, r, 1 - y if t == 2 else y))

    def y_copy(d, b, r, column):
        block = piece(b, d, r, owner(d, r, column), span(b, 0))
        return pltpu.make_async_remote_copy(
            src_ref=block, dst_ref=block, send_sem=y_s.at[d, b, r + 1], recv_sem=y_r.at[d, b, r + 1],
            device_id=across, device_id_type=MESH,
        )

    def a_copy(b, o):
        block = piece(b, 0, -1, o, span(b, 1))
        return pltpu.make_async_remote_copy(
            src_ref=block, dst_ref=block, send_sem=a_s.at[b], recv_sem=a_r.at[b],
            device_id=across, device_id_type=MESH,
        )

    def ways(r):
        return (0,) if r < 0 else (0, 1)

    def products(b, owners, fresh=False):
        first, count = BATCHES[b]
        rows = pl.ds(first * ROWS, count * ROWS)

        def one(d, _):
            for c in range(2):
                total = None
                for o in owners:
                    columns = pl.ds(pl.multiple_of(o * WIDTH, WIDTH), WIDTH)
                    block = gath[d, o, pl.ds(first, count)].reshape(count * ROWS, WIDTH)
                    term = lax.dot_general(
                        block, resp[c, d, :, columns], (((1,), (1,)), ((), ())),
                        preferred_element_type=jnp.float32,
                    )
                    total = term if total is None else total + term
                if fresh:
                    acc[d, c, rows, :] = total
                else:
                    acc[d, c, rows, :] += total
            return 0

        lax.fori_loop(0, NJ, one, 0)

    def begin(b):
        collect(b, 0, PLACES_A[b])
        a_copy(b, me).start()
        for d in range(2):
            z_send(d, 1, b, 0).start()
        collect(b, PLACES_A[b], CHIPS)
        for d in range(2):
            z_send(d, 0, b, 0).start()
        y_copy(0, b, -1, y).start()

    def begin_across(b):
        a_copy(b, partner).wait_recv()
        for d in range(2):
            z_send(d, 2, b, 0).start()
        products(b, [me], fresh=True)

    def owners_at(r, column):
        both = [owner(d, r, column) for d in ways(r)]
        return [partner] if r < 0 else both[:1] if r == FAR - 1 else both

    def step(b, r):
        for t in range(3):
            for d in range(2):
                z_recv(d, t, b, r).wait_recv()
                if r < FAR - 1:
                    z_send(d, t, b, r + 1).start()
                if t == 0:
                    y_copy(d, b, r, y).start()
        products(b, owners_at(r, y))

    def step_across(b, r):
        for d in ways(r):
            y_copy(d, b, r, 1 - y).wait_recv()
        products(b, owners_at(r, 1 - y))

    def back_copy(b, q):
        return pltpu.make_async_remote_copy(
            src_ref=back_out.at[groups_of(b), q], dst_ref=out_hbm.at[groups_of(b), f],
            send_sem=inv_s.at[b, q], recv_sem=inv_r.at[b, q],
            device_id=(ahead[q], me), device_id_type=MESH,
        )

    def keep_own(b):
        return pltpu.make_async_copy(back_out.at[groups_of(b), 0], out_hbm.at[groups_of(b), f], own_sem.at[b])

    def finish(b):
        sign = jnp.where(lax.broadcasted_iota(jnp.int32, (PEERS, PIECE, WIDTH), 1) < FEW, -1.0, 1.0)
        first, count = BATCHES[b]
        for g in range(first, first + count):
            rows = pl.ds(g * ROWS, ROWS)
            bins = []
            for j in range(NJ):
                straight = acc[j, 0, rows, :].reshape(PEERS, PIECE, WIDTH)
                turned = acc[j, 1, rows, :].reshape(PEERS, PIECE, WIDTH)
                bins.append(straight + sign * pltpu.roll(turned, FEW, 1))
            back_out[g] = jnp.concatenate(bins, axis=1).astype(jnp.bfloat16)
        for q in range(PEERS - 1, 0, -1):
            back_copy(b, q).start()
        keep_own(b).start()

    load_table.wait()
    for g in range(GROUPS):
        transform(g)
        if g == 0:
            load_resp.start()
            pl.semaphore_wait(barrier, len(peers))
        for b in batches:
            if sum(BATCHES[b]) == g + 1:
                spread(b)
    begin(0)
    load_resp.wait()
    begin_across(0)

    events = []
    for b in batches:
        if b > 0:
            events.append((STARTS[b] - LEADS[0], b, begin))
            events.append((STARTS[b] - LEADS[1], b, begin_across))
        for r in range(-1, FAR):
            if r >= 0:
                events.append((STARTS[b] + r, b, functools.partial(step, r=r)))
            events.append((STARTS[b] + r + LAG, b, functools.partial(step_across, r=r)))
        events.append((STARTS[b] + FAR - 1 + LAG, b, finish))
    for _, b, event in sorted(events, key=lambda e: e[:2]):
        event(b)

    for b in batches:
        keep_own(b).wait()
        a_copy(b, me).wait_send()
        for q in range(1, PEERS):
            back_copy(b, q).wait_recv()
            forward_copy(b, q).wait_send()
            back_copy(b, q).wait_send()
        for r in range(-1, FAR):
            for d in ways(r):
                y_copy(d, b, r, y).wait_send()
                for t in range(3):
                    if r >= 0:
                        z_send(d, t, b, r).wait_send()


def gather(response, focus_plus, table):
    bf16 = jnp.bfloat16
    dma = pltpu.SemaphoreType.DMA
    hbm = pl.BlockSpec(memory_space=pltpu.HBM)
    parts = len(BATCHES)
    return pl.pallas_call(
        gather_kernel,
        out_shape=jax.ShapeDtypeStruct((GROUPS, PEERS, TILE, WIDTH), bf16),
        in_specs=[hbm] * 3,
        out_specs=hbm,
        scratch_shapes=[
            pltpu.VMEM(response.shape, bf16),
            pltpu.VMEM(focus_plus.shape, bf16),
            pltpu.VMEM(table.shape, bf16),
            pltpu.VMEM((GROUPS, 2, HALF * FEW, LANES), jnp.float32),
            pltpu.VMEM((GROUPS, PEERS, TILE, WIDTH), bf16),
            pltpu.VMEM((GROUPS, PEERS, TILE, WIDTH), bf16),
            pltpu.VMEM((NJ, 2 * NZ, GROUPS, CHIPS, 2 * PIECE, WIDTH), bf16),
            pltpu.VMEM((NJ, 2, GROUPS * ROWS, WIDTH), jnp.float32),
            pltpu.VMEM((GROUPS, PEERS, TILE, WIDTH), bf16),
            dma((GROUPS + 2,)),
            dma((parts,)),
            dma((parts, PEERS)), dma((parts, PEERS)),
            dma((parts,)), dma((parts,)),
            dma((2, 3, parts, FAR)), dma((2, 3, parts, FAR)),
            dma((2, parts, FAR + 1)), dma((2, parts, FAR + 1)),
            dma((parts, PEERS)), dma((parts, PEERS)),
        ],
        compiler_params=pltpu.CompilerParams(
            collective_id=0, has_side_effects=True, vmem_limit_bytes=60 << 20
        ),
        name="gather",
    )(response, focus_plus, table)


def inverse_kernel(spectra_ref, table_ref, onset_ref, out_hbm, mine, out, sem):
    times = lax.broadcasted_iota(jnp.int32, (NT, WIDTH), 0)
    waves = table_ref[...]

    def store(i):
        return pltpu.make_async_copy(out.at[i], out_hbm.at[i], sem.at[i])

    for g in range(GROUPS):
        for h in range(2):
            rows = spectra_ref[g, :, :, pl.ds(h * LANES, LANES)].astype(jnp.float32)
            mine[g, h] = rows.reshape(HALF * FEW, LANES)
        for i in range(FEW):
            halves = [mine[g, h, pl.ds(i, HALF, stride=FEW), :] for h in range(2)]
            spectra = jnp.concatenate(halves, axis=1).astype(jnp.bfloat16)
            trace = jnp.dot(waves, spectra, preferred_element_type=jnp.float32)
            at = g * FEW + i
            out[at] = jnp.where(times < onset_ref[at : at + 1, :], trace, 0.0).astype(jnp.bfloat16)
            store(at).start()
    for i in range(FOCAL):
        store(i).wait()


def inverse(spectra, table, onset):
    vmem = pl.BlockSpec(memory_space=pltpu.VMEM)
    shape = (FOCAL, NT, WIDTH)
    return pl.pallas_call(
        inverse_kernel,
        out_shape=jax.ShapeDtypeStruct(shape, jnp.bfloat16),
        in_specs=[vmem] * 3,
        out_specs=pl.BlockSpec(memory_space=pltpu.HBM),
        scratch_shapes=[
            pltpu.VMEM((GROUPS, 2, HALF * FEW, LANES), jnp.float32),
            pltpu.VMEM(shape, jnp.bfloat16),
            pltpu.SemaphoreType.DMA((FOCAL,)),
        ],
        compiler_params=pltpu.CompilerParams(vmem_limit_bytes=60 << 20),
        name="inverse",
    )(spectra, table, onset)


def body(response, focus_plus, onset):
    forward_table, inverse_table = tables()
    spectra = gather(response, focus_plus, jnp.asarray(forward_table))
    return inverse(spectra, jnp.asarray(inverse_table), onset)


def solution(mesh):
    return jax.shard_map(
        body,
        mesh=mesh,
        in_specs=(P(None, "freq", "src", None), P("freq", None, "src"), P("freq", "src")),
        out_specs=P("freq", None, "src"),
        check_vma=False,
    )
```

time: 173 us -> 75 us (0.43)
  waiting for transfers between devices: 105 us -> 0 us
  Pallas kernels: 0 us -> 74.9 us
  blocking collectives: 18.3 us -> 0 us
  starting transfers between devices: 16.1 us -> 0 us
  matrix products: 13.6 us -> 0 us
  between operations: 13.5 us -> 0.01 us
  local copies, waits for them, and re-layouts: 5.08 us -> 0 us
    all_gather x1 -> x0, waiting for transfers between devices: 95.5 us -> none  [body(): piece = lax.all_gather(local, 'src', axis=3, tiled=True)]
    pallas_call x0 -> x2, Pallas kernels: none -> 74.9 us  [the longest x1 72.4 us: gather(): pl.pallas_call(gather_kernel, out_shape=jax.ShapeDtypeStruct((GROUPS, PEE...]
    all_to_all x1 -> x0, blocking collectives: 18.3 us -> none  [body(): lax.all_to_all(local, 'freq', split_axis=1, concat_axis=2, tiled=True)]
    all_to_all x1 -> x0, starting transfers between devices: 16.1 us -> none  [body(): lax.all_to_all(convolved, 'freq', split_axis=2, concat_axis=1, tiled=True)]
    dot_general x6 -> x0, matrix products: 13.6 us -> none  [the longest x1 4.81 us: body(): jnp.einsum('bsr,bxr->bxs', imag_r, imag_f, preferred_element_type=jnp.flo...]
    all_to_all x1 -> x0, waiting for transfers between devices: 9.87 us -> none  [body(): lax.all_to_all(convolved, 'freq', split_axis=2, concat_axis=1, tiled=True)]
    unnamed x10 -> x0, local copies, waits for them, and re-layouts: 1.9 us -> none
  transfers between devices with their start and end apart: 2 -> 0, of which waited for: 2 -> 0; matrix products, arithmetic and copies ran while one was open for 0% -> 0% of each run, Pallas kernels for 0% -> 0%
where the time goes in v3:
time: 75 us; the launch traced here: 74.9 us
  Pallas kernels  74.9 us (100%)
    pallas_call x1, Pallas kernels, gather(): pl.pallas_call(gather_kernel, out_shape=jax.ShapeDtypeStruct((GROUPS, PEE...  72.4 us
    pallas_call x1, Pallas kernels, inverse(): pl.pallas_call(inverse_kernel, out_shape=jax.ShapeDtypeStruct(shape, jnp....  2.5 us

profile of v3, /device:TPU:1, one launch (start us, length us, event | category | flops | bytes accessed | tf_op | source)
XLA Modules:
  0.0 74.9 jit_solution(5341896219760031776)
XLA Ops:
  0.0 72.4 %gather.1.spectra_ref = bf16[3,16,16,256]{3,2,1,0:T(8,128)(2,1)} custom-call(bf16[2,2,256,4096]{3,2,1,0:T(8,128)(2,1)} %resp_hbm.1, bf16[12,256,256]{2,1,0:T(8,128)(2,1)} %focus_hbm.1, bf16[64,256]{1,0:T(8,128)(2,1)} %constant.4.clone.table_hbm), custom_call_target="tpu_custom_call" | custom-call | tf_op jit(solution)/shard_map/gather/pallas_call | solution.py:304
  72.4 2.5 %inverse.1 = bf16[12,256,256]{2,1,0:T(8,128)(2,1)} custom-call(bf16[3,16,16,256]{3,2,1,0:T(8,128)(2,1)} %gather.1.spectra_ref, bf16[256,64]{1,0:T(8,128)(2,1)} %constant.5.clone.table_ref, s32[12,256]{1,0:T(8,128)} %onset_ref.1), custom_call_target="tpu_custom_call" | custom-call | tf_op jit(solution)/shard_map/inverse/pallas_call | solution.py:359

commit v4 on v3

--- a/solution.py
+++ b/solution.py
@@ -25,27 +25,30 @@
 PIECE = 2 * FEW
 ROWS = PEERS * PIECE
 HALF = NJ * 2 * PEERS
+TABLE = 1024
 NT = 256
 LANES = 128
 WIDTH = 256
 FAR = NZ // 2
 CHIP_PLACES = ((0, 0), (1, 0), (3, 0), (0, 1), (2, 0), (1, 1), (3, 1), (2, 1))
 PLACES = tuple((dx, dy, dc) for dx, dy in CHIP_PLACES for dc in range(2))
-BATCHES = ((0, 1), (1, 1), (2, 1))
-PLACES_A = (3, 3, 4)
-STARTS = (0.0, 0.2, 0.4)
+BATCHES = ((0, 3),)
+PLACES_A = (3,)
+AHEAD = 1.1
+STARTS = (0.0,)
 LEADS = (1.5, 0.5)
 LAG = 1.05
+OWN = len(BATCHES)
 
 
 def tables():
     samples = np.arange(NT, dtype=np.int32)
-    bins = (np.arange(HALF) // 2 + 1).astype(np.int32)
-    part = np.arange(HALF) % 2
+    bins = (np.arange(TABLE) // 2 + 1).astype(np.int32)
+    part = np.arange(TABLE) % 2
     phase = (bins[:, None] * samples) % NT
     angle = (np.float32(2.0 * math.pi) * phase.astype(np.float32) / np.float32(NT)).astype(np.float32)
     wave = np.where(part[:, None] == 0, np.cos(angle), -np.sin(angle)).astype(np.float32)
-    inverse = np.float32(2.0 / NT) * wave
+    inverse = np.float32(2.0 / NT) * wave[:HALF]
     return wave.astype(ml_dtypes.bfloat16), np.ascontiguousarray(inverse.T).astype(ml_dtypes.bfloat16)
 
 
@@ -78,7 +81,7 @@
     def load_focus(g):
         return pltpu.make_async_copy(few(focus_hbm, g), few(focus, g), load_sem.at[g])
 
-    load_table = pltpu.make_async_copy(table_hbm, table, load_sem.at[GROUPS])
+    load_table = pltpu.make_async_copy(table_hbm.at[pl.ds(0, HALF)], table, load_sem.at[GROUPS])
     load_resp = pltpu.make_async_copy(resp_hbm, resp, load_sem.at[GROUPS + 1])
     load_table.start()
     for g in range(GROUPS):
@@ -104,7 +107,7 @@
             blocks[g, :, :, pl.ds(h * LANES, LANES)] = rows
 
     def groups_of(b):
-        return pl.ds(*BATCHES[b])
+        return pl.ds(0, GROUPS) if b == OWN else pl.ds(*BATCHES[b])
 
     def forward_copy(b, q):
         return pltpu.make_async_remote_copy(
@@ -121,8 +124,9 @@
             arrived[g, 0] = blocks[g, f]
 
     def collect(b, first_chip, last_chip):
-        for q in range(max(1, 2 * first_chip), 2 * last_chip):
-            forward_copy(b, q).wait_recv()
+        for q in range(2 * first_chip, 2 * last_chip):
+            if q > 0:
+                forward_copy(b, q).wait_recv()
         first, count = BATCHES[b]
         for g in range(first, first + count):
             for p in range(first_chip, last_chip):
@@ -132,7 +136,9 @@
                     gath[j, me, g, p] = jnp.concatenate(rows, axis=0).astype(jnp.bfloat16)
 
     def span(b, t):
-        return pl.ds(0, PLACES_A[b]) if t else pl.ds(PLACES_A[b], CHIPS - PLACES_A[b])
+        if b == OWN:
+            return pl.ds(0, 1)
+        return pl.ds(1, PLACES_A[b]) if t else pl.ds(1 + PLACES_A[b], CHIPS - 1 - PLACES_A[b])
 
     def owner(d, r, column):
         return column * NZ + ((z + 2 * NZ - 1 - r) % NZ if d == 0 else (z + 1 + r) % NZ)
@@ -195,17 +201,26 @@
 
         lax.fori_loop(0, NJ, one, 0)
 
+    def begin_chip():
+        for b in batches:
+            collect(b, 0, 1)
+        for d in range(2):
+            z_send(d, 0, OWN, 0).start()
+        y_copy(0, OWN, -1, y).start()
+
     def begin(b):
-        collect(b, 0, PLACES_A[b])
+        collect(b, 1, 1 + PLACES_A[b])
         a_copy(b, me).start()
         for d in range(2):
             z_send(d, 1, b, 0).start()
-        collect(b, PLACES_A[b], CHIPS)
+        collect(b, 1 + PLACES_A[b], CHIPS)
         for d in range(2):
             z_send(d, 0, b, 0).start()
         y_copy(0, b, -1, y).start()
 
     def begin_across(b):
+        if b == 0:
+            load_resp.wait()
         a_copy(b, partner).wait_recv()
         for d in range(2):
             z_send(d, 2, b, 0).start()
@@ -216,19 +231,21 @@
         return [partner] if r < 0 else both[:1] if r == FAR - 1 else both
 
     def step(b, r):
-        for t in range(3):
+        for t in range(1 if b == OWN else 3):
             for d in range(2):
                 z_recv(d, t, b, r).wait_recv()
                 if r < FAR - 1:
                     z_send(d, t, b, r + 1).start()
                 if t == 0:
                     y_copy(d, b, r, y).start()
-        products(b, owners_at(r, y))
+        if b != OWN:
+            products(b, owners_at(r, y))
 
     def step_across(b, r):
         for d in ways(r):
             y_copy(d, b, r, 1 - y).wait_recv()
-        products(b, owners_at(r, 1 - y))
+        if b != OWN:
+            products(b, owners_at(r, 1 - y))
 
     def back_copy(b, q):
         return pltpu.make_async_remote_copy(
@@ -241,19 +258,19 @@
         return pltpu.make_async_copy(back_out.at[groups_of(b), 0], out_hbm.at[groups_of(b), f], own_sem.at[b])
 
     def finish(b):
-        sign = jnp.where(lax.broadcasted_iota(jnp.int32, (PEERS, PIECE, WIDTH), 1) < FEW, -1.0, 1.0)
+        sign = jnp.where(lax.broadcasted_iota(jnp.int32, (PIECE, WIDTH), 0) < FEW, -1.0, 1.0)
         first, count = BATCHES[b]
-        for g in range(first, first + count):
-            rows = pl.ds(g * ROWS, ROWS)
-            bins = []
-            for j in range(NJ):
-                straight = acc[j, 0, rows, :].reshape(PEERS, PIECE, WIDTH)
-                turned = acc[j, 1, rows, :].reshape(PEERS, PIECE, WIDTH)
-                bins.append(straight + sign * pltpu.roll(turned, FEW, 1))
-            back_out[g] = jnp.concatenate(bins, axis=1).astype(jnp.bfloat16)
-        for q in range(PEERS - 1, 0, -1):
-            back_copy(b, q).start()
-        keep_own(b).start()
+        for q in range(PEERS - 1, -1, -1):
+            for g in range(first, first + count):
+                rows = pl.ds(g * ROWS + q * PIECE, PIECE)
+                bins = [
+                    acc[j, 0, rows, :] + sign * pltpu.roll(acc[j, 1, rows, :], FEW, 0) for j in range(NJ)
+                ]
+                back_out[g, q] = jnp.concatenate(bins, axis=0).astype(jnp.bfloat16)
+            if q > 0:
+                back_copy(b, q).start()
+            else:
+                keep_own(b).start()
 
     load_table.wait()
     for g in range(GROUPS):
@@ -264,15 +281,17 @@
         for b in batches:
             if sum(BATCHES[b]) == g + 1:
                 spread(b)
-    begin(0)
-    load_resp.wait()
-    begin_across(0)
+    begin_chip()
 
     events = []
+    for r in range(-1, FAR):
+        if r >= 0:
+            events.append((STARTS[0] + r - AHEAD, OWN, functools.partial(step, r=r)))
+        events.append((STARTS[0] + r + LAG - AHEAD, OWN, functools.partial(step_across, r=r)))
     for b in batches:
-        if b > 0:
-            events.append((STARTS[b] - LEADS[0], b, begin))
-            events.append((STARTS[b] - LEADS[1], b, begin_across))
+        lead, lead_across = (0.5, 0.3) if b == 0 else LEADS
+        events.append((STARTS[b] - lead, b, begin))
+        events.append((STARTS[b] - lead_across, b, begin_across))
         for r in range(-1, FAR):
             if r >= 0:
                 events.append((STARTS[b] + r, b, functools.partial(step, r=r)))
@@ -288,10 +307,11 @@
             back_copy(b, q).wait_recv()
             forward_copy(b, q).wait_send()
             back_copy(b, q).wait_send()
+    for b in [*batches, OWN]:
         for r in range(-1, FAR):
             for d in ways(r):
                 y_copy(d, b, r, y).wait_send()
-                for t in range(3):
+                for t in range(1 if b == OWN else 3):
                     if r >= 0:
                         z_send(d, t, b, r).wait_send()
 
@@ -300,16 +320,16 @@
     bf16 = jnp.bfloat16
     dma = pltpu.SemaphoreType.DMA
     hbm = pl.BlockSpec(memory_space=pltpu.HBM)
-    parts = len(BATCHES)
+    parts = len(BATCHES) + 1
     return pl.pallas_call(
         gather_kernel,
         out_shape=jax.ShapeDtypeStruct((GROUPS, PEERS, TILE, WIDTH), bf16),
         in_specs=[hbm] * 3,
-        out_specs=hbm,
+        out_specs=pl.BlockSpec(memory_space=pl.ANY),
         scratch_shapes=[
             pltpu.VMEM(response.shape, bf16),
             pltpu.VMEM(focus_plus.shape, bf16),
-            pltpu.VMEM(table.shape, bf16),
+            pltpu.VMEM((HALF, NT), bf16),
             pltpu.VMEM((GROUPS, 2, HALF * FEW, LANES), jnp.float32),
             pltpu.VMEM((GROUPS, PEERS, TILE, WIDTH), bf16),
             pltpu.VMEM((GROUPS, PEERS, TILE, WIDTH), bf16),
@@ -325,7 +345,7 @@
             dma((parts, PEERS)), dma((parts, PEERS)),
         ],
         compiler_params=pltpu.CompilerParams(
-            collective_id=0, has_side_effects=True, vmem_limit_bytes=60 << 20
+            collective_id=0, has_side_effects=True, vmem_limit_bytes=63086592
         ),
         name="gather",
     )(response, focus_plus, table)
@@ -366,7 +386,7 @@
             pltpu.VMEM(shape, jnp.bfloat16),
             pltpu.SemaphoreType.DMA((FOCAL,)),
         ],
-        compiler_params=pltpu.CompilerParams(vmem_limit_bytes=60 << 20),
+        compiler_params=pltpu.CompilerParams(vmem_limit_bytes=8 << 20),
         name="inverse",
     )(spectra, table, onset)
 

time: 75 us -> 74.1 us (0.988)
  Pallas kernels: 74.9 us -> 72.9 us
  local copies, waits for them, and re-layouts: 0 us -> 1 us
    pallas_call x1, Pallas kernels: 2.5 us -> 1.47 us  [inverse(): pl.pallas_call(inverse_kernel, out_shape=jax.ShapeDtypeStruct(shape, jnp....]
    unnamed x0 -> x6, local copies, waits for them, and re-layouts: none -> 1 us
    pallas_call x1, Pallas kernels: 72.4 us -> 71.4 us  [gather(): pl.pallas_call(gather_kernel, out_shape=jax.ShapeDtypeStruct((GROUPS, PEE...]
where the time goes in v4:
time: 74.1 us; the launch traced here: 73.9 us
  Pallas kernels  72.9 us (98%)
  local copies, waits for them, and re-layouts  1 us (1%)
    pallas_call x1, Pallas kernels, gather(): pl.pallas_call(gather_kernel, out_shape=jax.ShapeDtypeStruct((GROUPS, PEE...  71.4 us

profile of v4, /device:TPU:1, one launch (start us, length us, event | category | flops | bytes accessed | tf_op | source)
XLA Modules:
  0.0 73.9 jit_solution(5987036544016409536)
XLA Ops:
  0.0 0.0 copy-start.1
  0.0 0.0 copy-start.2
  0.0 71.4 %gather.1.spectra_ref = bf16[3,16,16,256]{3,2,1,0:T(8,128)(2,1)} custom-call(bf16[2,2,256,4096]{3,2,1,0:T(8,128)(2,1)} %resp_hbm.1, bf16[12,256,256]{2,1,0:T(8,128)(2,1)} %focus_hbm.1, bf16[1024,256]{1,0:T(8,128)(2,1)} %constant.4.clone.table_hbm), custom_call_target="tpu_custom_call" | custom-call | tf_op jit(solution)/shard_map/gather/pallas_call | solution.py:324
  71.5 0.0 copy-done.1
  71.5 0.0 copy-done.2
  71.5 0.0 copy-start
  71.5 1.0 %copy-done = bf16[3,16,16,256]{3,2,1,0:T(8,128)(2,1)S(1)} copy-done((bf16[3,16,16,256]{3,2,1,0:T(8,128)(2,1)S(1)}, bf16[3,16,16,256]{3,2,1,0:T(8,128)(2,1)}, u32[]{:S(2)}) %copy-start) | copy-done | bytes 393240
  72.5 1.5 %inverse.1 = bf16[12,256,256]{2,1,0:T(8,128)(2,1)} custom-call(bf16[3,16,16,256]{3,2,1,0:T(8,128)(2,1)S(1)} %copy-done, bf16[256,64]{1,0:T(8,128)(2,1)S(1)} %copy-done.1, s32[12,256]{1,0:T(8,128)S(1)} %copy-done.2), custom_call_target="tpu_custom_call" | custom-call | tf_op jit(solution)/shard_map/inverse/pallas_call | solution.py:379
Async XLA Ops:
  0.0 71.5 %copy-start.1 = (bf16[256,64]{1,0:T(8,128)(2,1)S(1)}, bf16[256,64]{1,0:T(8,128)(2,1)}, u32[]{:S(2)}) copy-start(bf16[256,64]{1,0:T(8,128)(2,1)} %constant.5.clone.table_ref) | copy-start | bytes 98308
  0.0 71.5 %copy-start.2 = (s32[12,256]{1,0:T(8,128)S(1)}, s32[12,256]{1,0:T(8,128)}, u32[]{:S(2)}) copy-start(s32[12,256]{1,0:T(8,128)} %onset_ref.1) | copy-start | bytes 36868
  71.5 1.0 %copy-start = (bf16[3,16,16,256]{3,2,1,0:T(8,128)(2,1)S(1)}, bf16[3,16,16,256]{3,2,1,0:T(8,128)(2,1)}, u32[]{:S(2)}) copy-start(bf16[3,16,16,256]{3,2,1,0:T(8,128)(2,1)} %gather.1.spectra_ref) | copy-start | bytes 1179652

commit v5 on v4

--- a/solution.py
+++ b/solution.py
@@ -28,6 +28,7 @@
 TABLE = 1024
 NT = 256
 LANES = 128
+SPARE = 8
 WIDTH = 256
 FAR = NZ // 2
 CHIP_PLACES = ((0, 0), (1, 0), (3, 0), (0, 1), (2, 0), (1, 1), (3, 1), (2, 1))
@@ -103,7 +104,7 @@
 
         lax.fori_loop(0, FEW, one, 0)
         for h in range(2):
-            rows = mine[g, h].astype(jnp.bfloat16).reshape(PEERS, TILE, LANES)
+            rows = mine[g, h, : HALF * FEW, :].astype(jnp.bfloat16).reshape(PEERS, TILE, LANES)
             blocks[g, :, :, pl.ds(h * LANES, LANES)] = rows
 
     def groups_of(b):
@@ -330,7 +331,7 @@
             pltpu.VMEM(response.shape, bf16),
             pltpu.VMEM(focus_plus.shape, bf16),
             pltpu.VMEM((HALF, NT), bf16),
-            pltpu.VMEM((GROUPS, 2, HALF * FEW, LANES), jnp.float32),
+            pltpu.VMEM((GROUPS, 2, HALF * FEW + SPARE, LANES), jnp.float32),
             pltpu.VMEM((GROUPS, PEERS, TILE, WIDTH), bf16),
             pltpu.VMEM((GROUPS, PEERS, TILE, WIDTH), bf16),
             pltpu.VMEM((NJ, 2 * NZ, GROUPS, CHIPS, 2 * PIECE, WIDTH), bf16),
@@ -361,7 +362,7 @@
     for g in range(GROUPS):
         for h in range(2):
             rows = spectra_ref[g, :, :, pl.ds(h * LANES, LANES)].astype(jnp.float32)
-            mine[g, h] = rows.reshape(HALF * FEW, LANES)
+            mine[g, h, : HALF * FEW, :] = rows.reshape(HALF * FEW, LANES)
         for i in range(FEW):
             halves = [mine[g, h, pl.ds(i, HALF, stride=FEW), :] for h in range(2)]
             spectra = jnp.concatenate(halves, axis=1).astype(jnp.bfloat16)
@@ -382,7 +383,7 @@
         in_specs=[vmem] * 3,
         out_specs=pl.BlockSpec(memory_space=pltpu.HBM),
         scratch_shapes=[
-            pltpu.VMEM((GROUPS, 2, HALF * FEW, LANES), jnp.float32),
+            pltpu.VMEM((GROUPS, 2, HALF * FEW + SPARE, LANES), jnp.float32),
             pltpu.VMEM(shape, jnp.bfloat16),
             pltpu.SemaphoreType.DMA((FOCAL,)),
         ],

time: 74.1 us -> 74.1 us (level)
  no operation moved by 1% of the time
where the time goes in v5:
time: 74.1 us; the launch traced here: 74 us
  Pallas kernels  72.9 us (98%)
  local copies, waits for them, and re-layouts  1 us (1%)
    pallas_call x1, Pallas kernels, gather(): pl.pallas_call(gather_kernel, out_shape=jax.ShapeDtypeStruct((GROUPS, PEE...  71.5 us

profile of v5, /device:TPU:1, one launch (start us, length us, event | category | flops | bytes accessed | tf_op | source)
XLA Modules:
  0.0 74.0 jit_solution(4262645969673354622)
XLA Ops:
  0.0 0.0 copy-start.1
  0.0 0.0 copy-start.2
  0.0 71.5 %gather.1.spectra_ref = bf16[3,16,16,256]{3,2,1,0:T(8,128)(2,1)} custom-call(bf16[2,2,256,4096]{3,2,1,0:T(8,128)(2,1)} %resp_hbm.1, bf16[12,256,256]{2,1,0:T(8,128)(2,1)} %focus_hbm.1, bf16[1024,256]{1,0:T(8,128)(2,1)} %constant.4.clone.table_hbm), custom_call_target="tpu_custom_call" | custom-call | tf_op jit(solution)/shard_map/gather/pallas_call | solution.py:325
  71.5 0.0 copy-done.1
  71.5 0.0 copy-done.2
  71.5 0.0 copy-start
  71.5 1.0 %copy-done = bf16[3,16,16,256]{3,2,1,0:T(8,128)(2,1)S(1)} copy-done((bf16[3,16,16,256]{3,2,1,0:T(8,128)(2,1)S(1)}, bf16[3,16,16,256]{3,2,1,0:T(8,128)(2,1)}, u32[]{:S(2)}) %copy-start) | copy-done | bytes 393240
  72.5 1.5 %inverse.1 = bf16[12,256,256]{2,1,0:T(8,128)(2,1)} custom-call(bf16[3,16,16,256]{3,2,1,0:T(8,128)(2,1)S(1)} %copy-done, bf16[256,64]{1,0:T(8,128)(2,1)S(1)} %copy-done.1, s32[12,256]{1,0:T(8,128)S(1)} %copy-done.2), custom_call_target="tpu_custom_call" | custom-call | tf_op jit(solution)/shard_map/inverse/pallas_call | solution.py:380
Async XLA Ops:
  0.0 71.5 %copy-start.1 = (bf16[256,64]{1,0:T(8,128)(2,1)S(1)}, bf16[256,64]{1,0:T(8,128)(2,1)}, u32[]{:S(2)}) copy-start(bf16[256,64]{1,0:T(8,128)(2,1)} %constant.5.clone.table_ref) | copy-start | bytes 98308
  0.0 71.5 %copy-start.2 = (s32[12,256]{1,0:T(8,128)S(1)}, s32[12,256]{1,0:T(8,128)}, u32[]{:S(2)}) copy-start(s32[12,256]{1,0:T(8,128)} %onset_ref.1) | copy-start | bytes 36868
  71.5 1.0 %copy-start = (bf16[3,16,16,256]{3,2,1,0:T(8,128)(2,1)S(1)}, bf16[3,16,16,256]{3,2,1,0:T(8,128)(2,1)}, u32[]{:S(2)}) copy-start(bf16[3,16,16,256]{3,2,1,0:T(8,128)(2,1)} %gather.1.spectra_ref) | copy-start | bytes 1179652
